TPU v7x, 512 devices: a whole 4x8x8 slice. The times are simulated.
512 devices in a mesh: ctx: 32 (over y, x), dp: 16 (over z, core).
Axes of the slice: x: 4, y: 8, z: 8, core: 2. Of those that a mesh axis runs over, the one named last changes fastest.
Arguments:
- query_in: bfloat16 [16384, 8192], P('ctx', 'dp'), may hold values from -6 to 6
- key_in: bfloat16 [16384, 8192], P('ctx', 'dp'), may hold values from -6 to 6
- value_in: bfloat16 [16384, 8192], P('ctx', 'dp'), may hold values from -280 to 280
- log_decay: float32 [64, 16384], P('dp', 'ctx'), may hold values from -0.8 to 0
- norm_gain: float32 [8192], P('dp'), may hold values from 0.25 to 1.75
- grad_out: bfloat16 [16384, 8192], P('ctx', 'dp'), may hold values from -6 to 6
Outputs:
- attended: bfloat16 [16384, 8192], P('ctx', 'dp')
- grad_query: bfloat16 [16384, 8192], P('ctx', 'dp')
- grad_key: bfloat16 [16384, 8192], P('ctx', 'dp')
- grad_value: bfloat16 [16384, 8192], P('ctx', 'dp')
- grad_gain: float32 [8192], P('dp')
All inputs are finite; a program needn't handle non-finite values.
Results may differ from a plain program's by a relative error of at most 0.011.
Values sent between devices are 32-bit elements; how exact they have to be, the bound alone decides.
A program may use at most 64 MiB of HBM per device.

v0:
```python
import math

import jax
import jax.numpy as jnp
from jax import lax
from jax.sharding import PartitionSpec as P

BLOCK = 512


def entering(value, axis, join, neutral, backward):
    count, mine = (lax.axis_size(axis), lax.axis_index(axis))
    pieces = jax.tree.map(lambda part: lax.all_gather(part, axis), value)
    if backward:
        pieces = jax.tree.map(lambda part: part[::-1], pieces)
        mine = count - 1 - mine
    so_far = jax.tree.map(
        lambda part, zero: jnp.full_like(part, 0) + jnp.asarray(zero, part.dtype), value, neutral
    )

    def turn(position, so_far):
        longer = join(so_far, jax.tree.map(lambda part: part[position], pieces))
        return jax.tree.map(lambda new, old: jnp.where(position < mine, new, old), longer, so_far)

    return lax.fori_loop(0, count - 1, turn, so_far)


def chain_join(earlier, later):
    return (earlier[0] * later[0], later[0][:, None, None] * earlier[1] + later[1])


def split_product(form, left, state):
    high_part = state.astype(jnp.bfloat16)
    low_part = (state - high_part.astype(jnp.float32)).astype(jnp.bfloat16)
    first = jnp.einsum(form, left, high_part, preferred_element_type=jnp.float32)
    return first + jnp.einsum(form, left, low_part, preferred_element_type=jnp.float32)


def on_device(query_in, key_in, value_in, log_decay, norm_gain, grad_out):
    row_count = query_in.shape[0]
    head_count = log_decay.shape[0]
    head_width = query_in.shape[1] // head_count
    block_count = row_count // BLOCK
    shaped = (block_count, BLOCK, head_count, head_width)
    query_rows = query_in.reshape(shaped)
    key_rows = key_in.reshape(shaped)
    value_rows = value_in.reshape(shaped)
    within = jnp.transpose(
        jnp.cumsum(log_decay.reshape(head_count, block_count, BLOCK), axis=2), (1, 2, 0)
    )
    totals = within[:, -1, :]
    device_total = jnp.sum(totals, axis=0)
    decay_total = jnp.exp(device_total)
    within_heads = jnp.transpose(within, (0, 2, 1))
    causal_mask = jnp.arange(BLOCK)[:, None] >= jnp.arange(BLOCK)[None, :]
    decay_gap = within_heads[:, :, :, None] - within_heads[:, :, None, :]
    decay_weights = jnp.where(causal_mask, jnp.exp(jnp.where(causal_mask, decay_gap, 0.0)), 0.0)
    scores = jnp.einsum("nthd,nshd->nhts", query_rows, key_rows, preferred_element_type=jnp.float32)
    weighted = (scores * decay_weights).astype(jnp.bfloat16)
    local_mix = jnp.einsum(
        "nhts,nshj->nthj", weighted, value_rows, preferred_element_type=jnp.float32
    )
    tail_decay = jnp.exp(totals[:, None, :] - within)
    key_weighted = (key_rows.astype(jnp.float32) * tail_decay[..., None]).astype(jnp.bfloat16)
    block_states = jnp.einsum(
        "nshi,nshj->nhij", key_weighted, value_rows, preferred_element_type=jnp.float32
    )
    running = jnp.zeros_like(block_states[0])
    before = jnp.zeros_like(device_total)
    block_index = 0
    starts = running
    running = jnp.exp(totals[block_index])[:, None, None] * running + block_states[block_index]
    local_state = running
    incoming = entering(
        (decay_total, local_state),
        "ctx",
        chain_join,
        (jnp.ones_like(decay_total), jnp.zeros_like(local_state)),
        False,
    )[1]
    start_states = jnp.stack([starts + jnp.exp(before)[:, None, None] * incoming])
    within_exp = jnp.exp(within)[..., None]
    query_scaled = query_rows.astype(jnp.float32) * within_exp
    carried = within_exp * split_product("nthi,nhij->nthj", query_rows, start_states)
    raw_out = (carried + local_mix).reshape(row_count, -1)
    feature_total = head_count * head_width * lax.axis_size("dp")
    grad_float = grad_out.astype(jnp.float32)
    scaled_grad = grad_float * norm_gain
    square_sum, cross_sum = lax.psum(
        (jnp.sum(raw_out * raw_out, axis=1), jnp.sum(scaled_grad * raw_out, axis=1)), "dp"
    )
    inv_rms = lax.rsqrt(square_sum / feature_total + 1e-06)
    normed = raw_out * inv_rms[:, None]
    attended = (normed * norm_gain).astype(jnp.bfloat16)
    cubed = inv_rms * inv_rms * inv_rms
    grad_raw = (
        inv_rms[:, None] * scaled_grad
        - raw_out * cubed[:, None] * cross_sum[:, None] / feature_total
    ).astype(jnp.bfloat16)
    gain_part = jnp.sum(grad_float * normed, axis=0) / math.sqrt(row_count * lax.axis_size("ctx"))
    grad_rows = grad_raw.reshape(shaped)
    grad_scores = jnp.einsum(
        "nthj,nshj->nhts", grad_rows, value_rows, preferred_element_type=jnp.float32
    )
    grad_weighted = (grad_scores * decay_weights).astype(jnp.bfloat16)
    local_query = jnp.einsum(
        "nhts,nshi->nthi", grad_weighted, key_rows, preferred_element_type=jnp.float32
    )
    local_key = jnp.einsum(
        "nhts,nthi->nshi", grad_weighted, query_rows, preferred_element_type=jnp.float32
    )
    local_value = jnp.einsum(
        "nhts,nthj->nshj", weighted, grad_rows, preferred_element_type=jnp.float32
    )
    query_weighted = query_scaled.astype(jnp.bfloat16)
    back_blocks = jnp.einsum(
        "nuhi,nuhj->nhij", query_weighted, grad_rows, preferred_element_type=jnp.float32
    )
    afters = [None] * block_count
    after_sums = [None] * block_count
    running = jnp.zeros_like(back_blocks[0])
    behind = jnp.zeros_like(device_total)
    for block_index in reversed(range(block_count)):
        afters[block_index] = running
        after_sums[block_index] = behind
        running = jnp.exp(totals[block_index])[:, None, None] * running + back_blocks[block_index]
        behind = totals[block_index]
    back_in = entering(
        (decay_total, running),
        "ctx",
        chain_join,
        (jnp.ones_like(decay_total), jnp.zeros_like(running)),
        True,
    )[1]
    grad_gain = lax.psum(gain_part, "ctx")
    end_states = jnp.stack([afters[0] + jnp.exp(after_sums[0])[:, None, None] * back_in])
    query_carried = within_exp * split_product("nthj,nhij->nthi", grad_rows, start_states)
    key_carried = tail_decay[..., None] * split_product("nshj,nhij->nshi", value_rows, end_states)
    value_carried = tail_decay[..., None] * split_product("nshi,nhij->nshj", key_rows, end_states)
    grad_query = (query_carried + local_query).astype(jnp.bfloat16).reshape(row_count, -1)
    grad_key = (key_carried + local_key).astype(jnp.bfloat16).reshape(row_count, -1)
    grad_value = (value_carried + local_value).astype(jnp.bfloat16).reshape(row_count, -1)
    return (attended, grad_query, grad_key, grad_value, grad_gain)


def solution(mesh):
    in_specs = (
        P("ctx", "dp"),
        P("ctx", "dp"),
        P("ctx", "dp"),
        P("dp", "ctx"),
        P("dp"),
        P("ctx", "dp"),
    )
    out_specs = (P("ctx", "dp"), P("ctx", "dp"), P("ctx", "dp"), P("ctx", "dp"), P("dp"))
    return jax.shard_map(
        on_device, mesh=mesh, in_specs=in_specs, out_specs=out_specs, check_vma=False
    )
```

profile of v0, /device:TPU:1, one launch (start us, length us, event | category | flops | bytes accessed | tf_op | source)
XLA Modules:
  0.0 366.7 jit_solution(16275646209427864578)
XLA Ops:
  8.1 1.2 reduce-window.6
  10.2 1.3 copy.178
  12.8 31.4 %all-gather = f32[32,1,4]{2,1,0:T(1,128)S(1)} all-gather(f32[1,1,4]{2,1,0:T(1,128)S(1)} %get-tuple-element.303), channel_id=2, replica_groups=mesh['ctx'=32,'dp'=16] {'ctx'}, dimensions={0}, use_global_device_ids=true | all-gather | bytes 528 | tf_op jit(solution)/shard_map/all_gather | solution.py:13
  44.7 1.6 multiply_convert_fusion.1
  46.3 1.3 copy-done.1
  48.4 72.8 %all-gather.6.cloned.1.call-done = f32[128,128,128]{2,1,0:T(8,128)} async-done(((f32[4,128,128]{2,1,0:T(8,128)}), f32[128,128,128]{2,1,0:T(8,128)}) %all-gather.6.cloned.1.call-update) | async-done | bytes 8388624 | tf_op jit(solution)/shard_map/all_gather | solution.py:13
  121.2 34.0 %while.28 = (s32[]{:T(128)}, f32[4,128,128]{2,1,0:T(8,128)S(1)}, s32[]{:T(128)}, f32[32,4]{1,0:T(8,128)S(1)}, f32[32,4,128,128]{3,2,1,0:T(8,128)}, /*index=5*/s32[]{:T(128)}, s32[]{:T(128)}) while((s32[]{:T(128)}, f32[4,128,128]{2,1,0:T(8,128)S(1)}, s32[]{:T(128)}, f32[32,4]{1,0:T(8,128)S(1)}, f32[32,4,128,128]{3,2,1,0:T(8,128)}, ...), condition=%wide.region_3.4_spmd.clone, body=%wide.region_2.3_spmd.clone.sunk | while | flops 262148 | bytes 786593 | solution.py:25
  155.5 1.4 multiply_reduce_fusion
  156.9 25.1 %psum.21 = f32[512]{0:T(512)S(1)} all-reduce(f32[512]{0:T(512)S(1)} %get-tuple-element.306), channel_id=1, replica_groups=mesh['ctx'=32,'dp'=16] {'dp'}, use_global_device_ids=true, to_apply=%region_5.6 | all-reduce | flops 512 | bytes 4096 | tf_op jit(solution)/shard_map/psum | solution.py:89
  182.0 1.6 copy.110
  184.0 25.4 %psum.22 = f32[512]{0:T(512)S(1)} all-reduce(f32[512]{0:T(512)S(1)} %get-tuple-element.277), channel_id=1, replica_groups=mesh['ctx'=32,'dp'=16] {'dp'}, use_global_device_ids=true, to_apply=%region_7.8 | all-reduce | flops 512 | bytes 4096 | tf_op jit(solution)/shard_map/psum | solution.py:89
  209.4 1.4 fusion.20
  210.8 1.3 copy.141
  213.3 2.6 multiply_convert_fusion
  218.3 58.3 %psum.23 = f32[512]{0:T(512)} all-reduce(f32[512]{0:T(512)S(1)} %broadcast_multiply_fusion), channel_id=1, replica_groups=mesh['ctx'=32,'dp'=16] {'ctx'}, use_global_device_ids=true, to_apply=%region_11.12 | all-reduce | flops 512 | bytes 4096 | tf_op jit(solution)/shard_map/psum | solution.py:135
  276.7 3.2 convolution_bitcast_fusion.1
  280.3 30.8 %all-gather.8.cloned.1.call-done = f32[128,128,128]{2,1,0:T(8,128)} async-done(((f32[4,128,128]{2,1,0:T(8,128)}), f32[128,128,128]{2,1,0:T(8,128)}) %all-gather.8.cloned.1.call-update) | async-done | bytes 8388624 | tf_op jit(solution)/shard_map/all_gather | solution.py:13
  311.1 7.8 %rev.7 = f32[32,4,128,128]{3,2,1,0:T(8,128)} reverse(f32[32,4,128,128]{3,2,1,0:T(8,128)} %bitcast.197), dimensions={0} | reverse | bytes 16777216 | tf_op jit(solution)/shard_map/rev | solution.py:15
  318.9 34.1 %while.29 = (s32[]{:T(128)}, f32[4,128,128]{2,1,0:T(8,128)S(1)}, s32[]{:T(128)}, f32[32,4]{1,0:T(8,128)S(1)}, f32[32,4,128,128]{3,2,1,0:T(8,128)}, /*index=5*/s32[]{:T(128)}, s32[]{:T(128)}) while((s32[]{:T(128)}, f32[4,128,128]{2,1,0:T(8,128)S(1)}, s32[]{:T(128)}, f32[32,4]{1,0:T(8,128)S(1)}, f32[32,4,128,128]{3,2,1,0:T(8,128)}, ...), condition=%wide.region_9.10_spmd.clone, body=%wide.region_8.9_spmd.clone.sunk | while | flops 262148 | bytes 786593 | solution.py:25
  320.0 1.1 fusion.75
  321.1 1.1 fusion.75
  322.2 1.1 fusion.75
  323.3 1.1 fusion.75
  324.4 1.1 fusion.75
  325.5 1.1 fusion.75
  326.6 1.1 fusion.75
  327.7 1.1 fusion.75
  344.3 1.1 fusion.75
  348.7 1.1 fusion.75
  353.4 1.3 fusion.29
  354.7 1.6 fusion.14
  357.3 1.5 fusion.15
  (177 shorter events, 67.1 us)
Async XLA Ops:
  7.2 4.3 %copy-start = (bf16[512,512]{1,0:T(8,128)(2,1)S(1)}, bf16[512,512]{1,0:T(8,128)(2,1)}, u32[]{:S(2)}) copy-start(bf16[512,512]{1,0:T(8,128)(2,1)} %param.12) | copy-start | bytes 1572868
  7.2 37.5 %copy-start.4 = (bf16[512,512]{1,0:T(8,128)(2,1)S(1)}, bf16[512,512]{1,0:T(8,128)(2,1)}, u32[]{:S(2)}) copy-start(bf16[512,512]{1,0:T(8,128)(2,1)} %param.11) | copy-start | bytes 1572868
  7.2 37.1 %copy-start.8 = (bf16[512,512]{1,0:T(8,128)(2,1)S(1)}, bf16[512,512]{1,0:T(8,128)(2,1)}, u32[]{:S(2)}) copy-start(bf16[512,512]{1,0:T(8,128)(2,1)} %param.10) | copy-start | bytes 1572868
  7.2 114.0 %all-gather.6.cloned.1.call-start = ((), (), s32[]{:S(2)}) async-start(), calls=%async_computation | async-start | bytes 8650752 | tf_op jit(solution)/shard_map/all_gather | solution.py:13
  11.4 32.8 %copy-start.6 = (bf16[512,512]{0,1:T(8,128)(2,1)}, bf16[512,512]{0,1:T(8,128)(2,1)S(1)}, u32[]{:S(2)}) copy-start(bf16[512,512]{0,1:T(8,128)(2,1)S(1)} %copy.178) | copy-start | bytes 1572868
  12.5 298.6 %all-gather.8.cloned.1.call-start = ((), (), s32[]{:S(2)}) async-start(), calls=%async_computation.1 | async-start | bytes 8650752 | tf_op jit(solution)/shard_map/all_gather | solution.py:13
  44.6 1.6 copy-start.9
  46.2 1.3 copy-start.1
  155.2 28.4 %copy-start.5 = (bf16[512,512]{1,0:T(8,128)(2,1)S(1)}, bf16[512,512]{1,0:T(8,128)(2,1)}, u32[]{:S(2)}) copy-start(bf16[512,512]{1,0:T(8,128)(2,1)} %param.15) | copy-start | bytes 1572868
  155.2 28.4 %copy-start.10 = (f32[512]{0:T(512)S(1)}, f32[512]{0:T(512)}, u32[]{:S(2)}) copy-start(f32[512]{0:T(512)} %param.14) | copy-start | bytes 6148
  213.3 2.6 copy-start.7
  215.9 1.4 copy-start.2
  276.6 3.2 copy-start.3
Sparse Core Ops, SparseCore 0:
  12.6 108.5 all-gather.5
  213.2 97.8 all-gather.7
where the time goes:
time: 369 us; the launch traced here: 367 us
  blocking collectives  140 us (38%)
  waiting for transfers between devices  104 us (28%)
  other arithmetic  68.9 us (19%)
  local copies, waits for them, and re-layouts  19.1 us (5%)
  matrix products  18.5 us (5%)
  between operations  14.4 us (4%)
    all_gather x2, waiting for transfers between devices, entering(): pieces = jax.tree.map(lambda part: lax.all_gather(part, axis), value)  104 us
    select_n x62, other arithmetic, turn(): jnp.where(position < mine, new, old)  65.5 us
    psum x1, blocking collectives, on_device(): grad_gain = lax.psum(gain_part, 'ctx')  58.3 us
    psum x2, blocking collectives, on_device(): lax.psum((jnp.sum(raw_out * raw_out, axis=1), jnp.sum(scaled_grad * raw_o...  50.5 us
    all_gather x1, blocking collectives, entering(): pieces = jax.tree.map(lambda part: lax.all_gather(part, axis), value)  31.4 us
    rev x2, local copies, waits for them, and re-layouts, entering(): pieces = jax.tree.map(lambda part: part[::-1], pieces)  7.89 us
  transfers between devices with their start and end apart: 2, of which 2 were waited for; matrix products, arithmetic and copies ran while one was open for 3% of the time, Pallas kernels for 0%

commit v1 on v0

v1 whole, which is shorter than its diff:
```python
import functools
import math

import jax
import jax.numpy as jnp
from jax import lax
from jax.experimental import pallas as pl
from jax.experimental.pallas import tpu as pltpu
from jax.sharding import PartitionSpec as P

MESH = pl.DeviceIdType.MESH
HEAD = 128
HEADS_HERE = 4
CHUNK = 128
CHUNKS = 4
ROWS = CHUNK * CHUNKS
EXTRA = 8
RING_X = 4

NT = (((1,), (1,)), ((), ()))
NN = (((1,), (0,)), ((), ()))
TN = (((0,), (0,)), ((), ()))


def mxu(left, right, form):
    return lax.dot_general(left, right, form, preferred_element_type=jnp.float32)


def split(state):
    high = state.astype(jnp.bfloat16)
    return high, (state - high.astype(jnp.float32)).astype(jnp.bfloat16)


def part(index):
    return slice(index * CHUNK, (index + 1) * CHUNK)


def kernel(
    n_ctx,
    n_dp,
    ring_x,
    q_ref,
    k_ref,
    v_ref,
    decay_ref,
    gain_ref,
    go_ref,
    attended_ref,
    gq_ref,
    gk_ref,
    gv_ref,
    gg_ref,
    rows_ref,
    cols_ref,
    gap_ref,
    weighted_ref,
    gw_ref,
    mix_ref,
    g_ref,
    qw_ref,
    lk_ref,
    lv_ref,
    send_f,
    recv_f,
    back_f,
    start_ref,
    send_b,
    recv_b,
    back_b,
    end_ref,
    sums_ref,
    norm_cols_ref,
    sems_f,
    semr_f,
    sems_fb,
    semr_fb,
    sems_b,
    semr_b,
    sems_bb,
    semr_bb,
    sems_n,
    semr_n,
):
    me = lax.axis_index("ctx")
    col = lax.axis_index("dp")
    piece = ROWS // n_ctx
    per_head = HEAD // piece
    ring_y = n_ctx // ring_x
    my_y, my_x = me // ring_x, me % ring_x

    barrier = pltpu.get_barrier_semaphore()

    def greet_ctx(i, carry):
        pl.semaphore_signal(
            barrier, inc=1, device_id={"ctx": (me + i) % n_ctx}, device_id_type=MESH
        )
        return carry

    def greet_dp(i, carry):
        pl.semaphore_signal(
            barrier, inc=1, device_id={"dp": (col + i) % n_dp}, device_id_type=MESH
        )
        return carry

    lax.fori_loop(1, n_ctx, greet_ctx, 0)
    lax.fori_loop(1, n_dp, greet_dp, 0)

    logs = decay_ref[...]
    stacked = jnp.concatenate([logs[:, part(c)] for c in range(CHUNKS)], axis=0)
    high = stacked.astype(jnp.bfloat16)
    rest = stacked - high.astype(jnp.float32)
    middle = rest.astype(jnp.bfloat16)
    low = (rest - middle.astype(jnp.float32)).astype(jnp.bfloat16)
    row_i = lax.broadcasted_iota(jnp.int32, (CHUNK, 2 * CHUNK), 0)
    col_i = lax.broadcasted_iota(jnp.int32, (CHUNK, 2 * CHUNK), 1)
    adder = jnp.where(row_i <= col_i, 1.0, 0.0).astype(jnp.bfloat16)
    sums = mxu(jnp.concatenate([high, middle, low], axis=0), adder, NN)
    sums = sums[0:16] + sums[16:32] + sums[32:48]
    inside, chunk_total = sums[:, :CHUNK], sums[:, CHUNK:]
    before = jnp.zeros((HEADS_HERE, CHUNK), jnp.float32)
    within = []
    for c in range(CHUNKS):
        block = slice(c * HEADS_HERE, (c + 1) * HEADS_HERE)
        within.append(inside[block] + before)
        before = before + chunk_total[block]
    total = before
    within = jnp.concatenate(within, axis=0)
    tail = jnp.exp(jnp.concatenate([total] * CHUNKS, axis=0) - within)
    rows_ref[...] = within
    cols_ref[...] = jnp.concatenate(
        [within, jnp.exp(within), tail, jnp.zeros((CHUNK - 48, CHUNK), jnp.float32)],
        axis=0,
    ).T

    def column(kind, h, c):
        at = 16 * kind + c * HEADS_HERE + h
        return cols_ref[:, at : at + 1]

    for h in range(HEADS_HERE):
        weighted_keys = jnp.concatenate(
            [
                (k_ref[part(c), part(h)].astype(jnp.float32) * column(2, h, c)).astype(
                    jnp.bfloat16
                )
                for c in range(CHUNKS)
            ],
            axis=0,
        )
        state = mxu(weighted_keys, v_ref[:, part(h)], TN)
        send_f[h * per_head : (h + 1) * per_head, :piece, :] = state.reshape(
            per_head, piece, HEAD
        )
        send_f[h * per_head : (h + 1) * per_head, piece:, :] = jnp.broadcast_to(
            total[h : h + 1][None], (per_head, EXTRA, HEAD)
        )
    recv_f[pl.ds(me, 1)] = send_f[pl.ds(me, 1)]

    pl.semaphore_wait(barrier, n_ctx - 1 + n_dp - 1)

    def far_first(i):
        k, j = i // ring_x, i % ring_x
        step_y = ring_y // 2 + ((k + 1) // 2) * (1 - 2 * ((k + 1) % 2))
        step_x = ring_x // 2 + ((j + 1) // 2) * (1 - 2 * ((j + 1) % 2))
        return ((my_y + step_y) % ring_y) * ring_x + (my_x + step_x) % ring_x

    def out_copy(there, send, recv, ss, rs):
        return pltpu.make_async_remote_copy(
            src_ref=send.at[there],
            dst_ref=recv.at[me],
            send_sem=ss.at[there],
            recv_sem=rs.at[me],
            device_id={"ctx": there},
            device_id_type=MESH,
        )

    def in_copy(there, send, recv, ss, rs):
        return pltpu.make_async_remote_copy(
            src_ref=send.at[there],
            dst_ref=recv.at[there],
            send_sem=ss.at[there],
            recv_sem=rs.at[there],
            device_id={"ctx": there},
            device_id_type=MESH,
        )

    def spread(send, recv, ss, rs):
        def one(i, carry):
            out_copy(far_first(i), send, recv, ss, rs).start()
            return carry

        lax.fori_loop(0, n_ctx - 1, one, 0)

    def wait_sent(send, recv, ss, rs):
        def one(i, carry):
            there = (me + i) % n_ctx
            in_copy(there, send, recv, ss, rs).wait_send()
            return carry

        lax.fori_loop(1, n_ctx, one, 0)

    def wait_pieces(first, last, send, recv, ss, rs):
        def one(there, carry):
            @pl.when(there != me)
            def _():
                in_copy(there, send, recv, ss, rs).wait_recv()

            return carry

        lax.fori_loop(first, last, one, 0)

    spread(send_f, recv_f, sems_f, semr_f)

    diag_t = lax.broadcasted_iota(jnp.int32, (CHUNK, CHUNK), 0)
    diag_s = lax.broadcasted_iota(jnp.int32, (CHUNK, CHUNK), 1)

    def forward_part(h):
        for i in range(CHUNKS):
            scores = mxu(
                q_ref[part(i), part(h)], k_ref[: (i + 1) * CHUNK, part(h)], NT
            )
            here = column(0, h, i)
            for j in range(i + 1):
                at = j * HEADS_HERE + h
                gap = here - rows_ref[at : at + 1, :]
                if i == j:
                    gap = jnp.where(diag_t >= diag_s, gap, -1e30)
                weight = jnp.exp(gap)
                gap_ref[h, part(i), part(j)] = weight
                weighted_ref[h, part(i), part(j)] = (
                    scores[:, part(j)] * weight
                ).astype(jnp.bfloat16)
            mix_ref[part(i), part(h)] = mxu(
                weighted_ref[h, part(i), : (i + 1) * CHUNK],
                v_ref[: (i + 1) * CHUNK, part(h)],
                NN,
            )
            qw_ref[part(i), part(h)] = (
                q_ref[part(i), part(h)].astype(jnp.float32) * column(1, h, i)
            ).astype(jnp.bfloat16)

    forward_part(0)
    forward_part(1)

    def scan_forward(there, running):
        @pl.when(there != me)
        def _():
            in_copy(there, send_f, recv_f, sems_f, semr_f).wait_recv()

        back_f[pl.ds(there, 1)] = running[None]

        @pl.when(there != me)
        def _():
            out_copy(there, back_f, start_ref, sems_fb, semr_fb).start()

        arrived = recv_f[pl.ds(there, 1)][0]
        return jnp.exp(arrived[piece : piece + 1]) * running + arrived[:piece]

    lax.fori_loop(0, n_ctx, scan_forward, jnp.zeros((piece, HEAD), jnp.float32))
    start_ref[pl.ds(me, 1)] = back_f[pl.ds(me, 1)]

    forward_part(2)
    forward_part(3)

    for h in range(HEADS_HERE):
        wait_pieces(
            h * per_head, (h + 1) * per_head, back_f, start_ref, sems_fb, semr_fb
        )
        start = start_ref[h * per_head : (h + 1) * per_head].reshape(HEAD, HEAD)
        high, low = split(start)
        for c in range(CHUNKS):
            rows = q_ref[part(c), part(h)]
            carried = mxu(rows, high, NN) + mxu(rows, low, NN)
            mix_ref[part(c), part(h)] += column(1, h, c) * carried

    ones = jnp.ones((8, CHUNK), jnp.float32)

    def row_sums(terms):
        return lax.dot_general(
            ones,
            terms,
            NT,
            preferred_element_type=jnp.float32,
            precision=lax.Precision.HIGHEST,
        )[0:1]

    squares, crosses = [], []
    for c in range(CHUNKS):
        square = jnp.zeros((CHUNK, HEAD), jnp.float32)
        cross = jnp.zeros((CHUNK, HEAD), jnp.float32)
        for h in range(HEADS_HERE):
            raw = mix_ref[part(c), part(h)]
            square += raw * raw
            cross += (
                go_ref[part(c), part(h)].astype(jnp.float32) * gain_ref[:, part(h)]
            ) * raw
        squares.append(row_sums(square))
        crosses.append(row_sums(cross))
    sums_ref[pl.ds(col, 1)] = jnp.concatenate(squares + crosses, axis=0)[None]

    def norm_copy(slot, there):
        return pltpu.make_async_remote_copy(
            src_ref=sums_ref.at[slot],
            dst_ref=sums_ref.at[slot],
            send_sem=sems_n.at[there],
            recv_sem=semr_n.at[slot],
            device_id={"dp": there},
            device_id_type=MESH,
        )

    def norm_send(i, carry):
        norm_copy(col, (col + n_dp // 2 + i) % n_dp).start()
        return carry

    def norm_wait(i, carry):
        there = (col + i) % n_dp
        norm_copy(there, there).wait_recv()
        return carry

    half = n_dp // 2
    lax.fori_loop(0, half, norm_send, 0)
    lax.fori_loop(half + 1, n_dp, norm_send, 0)
    lax.fori_loop(1, n_dp, norm_wait, 0)

    both = jnp.sum(sums_ref[...], axis=0)
    features = HEAD * HEADS_HERE * n_dp
    inv = lax.rsqrt(both[:CHUNKS] / features + 1e-06)
    bent = inv * inv * inv * both[CHUNKS:] / features
    norm_cols_ref[...] = jnp.concatenate(
        [inv, bent, jnp.zeros((CHUNK - 8, CHUNK), jnp.float32)], axis=0
    ).T

    scale = 1.0 / math.sqrt(ROWS * n_ctx)
    for h in range(HEADS_HERE):
        gain = gain_ref[:, part(h)]
        gain_part = jnp.zeros((1, HEAD), jnp.float32)
        for c in range(CHUNKS):
            raw = mix_ref[part(c), part(h)]
            grad = go_ref[part(c), part(h)].astype(jnp.float32)
            inv_c = norm_cols_ref[:, c : c + 1]
            bent_c = norm_cols_ref[:, CHUNKS + c : CHUNKS + c + 1]
            normed = raw * inv_c
            attended_ref[part(c), part(h)] = (normed * gain).astype(jnp.bfloat16)
            gain_part += jnp.sum(grad * normed, axis=0, keepdims=True)
            g_ref[part(c), part(h)] = (inv_c * (grad * gain) - raw * bent_c).astype(
                jnp.bfloat16
            )
        back = mxu(qw_ref[:, part(h)], g_ref[:, part(h)], TN)
        send_b[h * per_head : (h + 1) * per_head, :piece, :] = back.reshape(
            per_head, piece, HEAD
        )
        send_b[h * per_head : (h + 1) * per_head, piece:, :] = jnp.broadcast_to(
            (gain_part * scale)[None], (per_head, EXTRA, HEAD)
        )
    recv_b[pl.ds(me, 1)] = send_b[pl.ds(me, 1)]
    spread(send_b, recv_b, sems_b, semr_b)

    def backward_part(h):
        start = start_ref[h * per_head : (h + 1) * per_head].reshape(HEAD, HEAD)
        high, low = split(start)
        for i in range(CHUNKS):
            upto = slice(0, (i + 1) * CHUNK)
            rows = g_ref[part(i), part(h)]
            scores = mxu(rows, v_ref[upto, part(h)], NT)
            for j in range(i + 1):
                gw_ref[h, part(i), part(j)] = (
                    scores[:, part(j)] * gap_ref[h, part(i), part(j)]
                ).astype(jnp.bfloat16)
            local = mxu(gw_ref[h, part(i), upto], k_ref[upto, part(h)], NN)
            carried = mxu(rows, high, NT) + mxu(rows, low, NT)
            gq_ref[part(i), part(h)] = (column(1, h, i) * carried + local).astype(
                jnp.bfloat16
            )
        for j in range(CHUNKS):
            down = slice(j * CHUNK, ROWS)
            lk_ref[part(j), part(h)] = mxu(
                gw_ref[h, down, part(j)], q_ref[down, part(h)], TN
            )
            lv_ref[part(j), part(h)] = mxu(
                weighted_ref[h, down, part(j)], g_ref[down, part(h)], TN
            )

    backward_part(0)
    backward_part(1)

    def scan_backward(i, carry):
        running, gain_sum = carry
        there = n_ctx - 1 - i

        @pl.when(there != me)
        def _():
            in_copy(there, send_b, recv_b, sems_b, semr_b).wait_recv()

        back_b[pl.ds(there, 1), :piece] = running[None]
        arrived = recv_b[pl.ds(there, 1)][0]
        decay = jnp.exp(recv_f[pl.ds(there, 1)][0, piece : piece + 1])
        return decay * running + arrived[:piece], gain_sum + arrived[piece:]

    _, gain_sum = lax.fori_loop(
        0,
        n_ctx,
        scan_backward,
        (jnp.zeros((piece, HEAD), jnp.float32), jnp.zeros((EXTRA, HEAD), jnp.float32)),
    )

    def gain_out(there, carry):
        back_b[pl.ds(there, 1), piece:] = gain_sum[None]

        @pl.when(there != me)
        def _():
            out_copy(there, back_b, end_ref, sems_bb, semr_bb).start()

        return carry

    lax.fori_loop(0, n_ctx, gain_out, 0)
    end_ref[pl.ds(me, 1)] = back_b[pl.ds(me, 1)]

    backward_part(2)
    backward_part(3)

    for h in range(HEADS_HERE):
        wait_pieces(
            h * per_head, (h + 1) * per_head, back_b, end_ref, sems_bb, semr_bb
        )
        end = end_ref[h * per_head : (h + 1) * per_head, :piece].reshape(HEAD, HEAD)
        gg_ref[:, part(h)] = end_ref[h * per_head, piece : piece + 1]
        high, low = split(end)
        for c in range(CHUNKS):
            values, keys = v_ref[part(c), part(h)], k_ref[part(c), part(h)]
            fade = column(2, h, c)
            key_carried = mxu(values, high, NT) + mxu(values, low, NT)
            value_carried = mxu(keys, high, NN) + mxu(keys, low, NN)
            gk_ref[part(c), part(h)] = (
                fade * key_carried + lk_ref[part(c), part(h)]
            ).astype(jnp.bfloat16)
            gv_ref[part(c), part(h)] = (
                fade * value_carried + lv_ref[part(c), part(h)]
            ).astype(jnp.bfloat16)

    wait_sent(send_f, recv_f, sems_f, semr_f)
    wait_sent(back_f, start_ref, sems_fb, semr_fb)
    wait_sent(send_b, recv_b, sems_b, semr_b)
    wait_sent(back_b, end_ref, sems_bb, semr_bb)

    def norm_sent(i, carry):
        there = (col + i) % n_dp
        norm_copy(col, there).wait_send()
        return carry

    lax.fori_loop(1, n_dp, norm_sent, 0)


def on_device(
    n_ctx, n_dp, ring_x, query_in, key_in, value_in, log_decay, norm_gain, grad_out
):
    width = HEAD * HEADS_HERE
    piece = ROWS // n_ctx
    full = jax.ShapeDtypeStruct((ROWS, width), jnp.bfloat16)
    f32, bf16 = jnp.float32, jnp.bfloat16
    message = pltpu.VMEM((n_ctx, piece + EXTRA, HEAD), f32)
    plain = pltpu.VMEM((n_ctx, piece, HEAD), f32)
    vmem = pl.BlockSpec(memory_space=pltpu.VMEM)
    outs = pl.pallas_call(
        functools.partial(kernel, n_ctx, n_dp, ring_x),
        out_shape=[full] * 4 + [jax.ShapeDtypeStruct((1, width), f32)],
        in_specs=[vmem] * 6,
        out_specs=[vmem] * 5,
        scratch_shapes=[
            pltpu.VMEM((16, CHUNK), f32),
            pltpu.VMEM((CHUNK, CHUNK), f32),
            pltpu.VMEM((HEADS_HERE, ROWS, ROWS), f32),
            pltpu.VMEM((HEADS_HERE, ROWS, ROWS), bf16),
            pltpu.VMEM((HEADS_HERE, ROWS, ROWS), bf16),
            pltpu.VMEM((ROWS, width), f32),
            pltpu.VMEM((ROWS, width), bf16),
            pltpu.VMEM((ROWS, width), bf16),
            pltpu.VMEM((ROWS, width), f32),
            pltpu.VMEM((ROWS, width), f32),
            message,
            message,
            plain,
            plain,
            message,
            message,
            message,
            message,
            pltpu.VMEM((n_dp, 8, CHUNK), f32),
            pltpu.VMEM((CHUNK, CHUNK), f32),
        ]
        + [pltpu.SemaphoreType.DMA((n_ctx,))] * 8
        + [pltpu.SemaphoreType.DMA((n_dp,))] * 2,
        compiler_params=pltpu.CompilerParams(
            collective_id=0,
            has_side_effects=True,
            vmem_limit_bytes=40 * 1024 * 1024,
        ),
        name="lightning",
    )(
        query_in,
        key_in,
        value_in,
        log_decay,
        norm_gain.reshape(1, width),
        grad_out,
    )
    return (*outs[:4], outs[4].reshape(width))


def solution(mesh):
    in_specs = (
        P("ctx", "dp"),
        P("ctx", "dp"),
        P("ctx", "dp"),
        P("dp", "ctx"),
        P("dp"),
        P("ctx", "dp"),
    )
    out_specs = (P("ctx", "dp"), P("ctx", "dp"), P("ctx", "dp"), P("ctx", "dp"), P("dp"))
    n_ctx, n_dp = mesh.shape["ctx"], mesh.shape["dp"]
    return jax.shard_map(
        functools.partial(on_device, n_ctx, n_dp, min(RING_X, n_ctx // 2)),
        mesh=mesh,
        in_specs=in_specs,
        out_specs=out_specs,
        check_vma=False,
    )
```

time: 369 us -> 80.2 us (0.22)
  the two profiles are of different devices: /device:TPU:1 before, /device:TPU:16 now
where the time goes in v1:
time: 80.2 us; the launch traced here: 79.8 us
  Pallas kernels  69.9 us (87%)
  local copies, waits for them, and re-layouts  9.29 us (12%)
    pallas_call x1, Pallas kernels, on_device(): pl.pallas_call(functools.partial(kernel, n_ctx, n_dp, ring_x), out_shape=...  69.9 us
    unnamed x17, local copies, waits for them, and re-layouts  9.29 us

profile of v1, /device:TPU:16, one launch (start us, length us, event | category | flops | bytes accessed | tf_op | source)
XLA Modules:
  0.0 79.8 jit_solution(4631348837760382166)
XLA Ops:
  0.6 0.0 copy-start
  0.6 1.0 %copy-done = bf16[512,512]{1,0:T(8,128)(2,1)S(1)} copy-done((bf16[512,512]{1,0:T(8,128)(2,1)S(1)}, bf16[512,512]{1,0:T(8,128)(2,1)}, u32[]{:S(2)}) %copy-start) | copy-done | bytes 524312
  1.7 0.0 copy-start.1
  1.7 1.0 %copy-done.1 = bf16[512,512]{1,0:T(8,128)(2,1)S(1)} copy-done((bf16[512,512]{1,0:T(8,128)(2,1)S(1)}, bf16[512,512]{1,0:T(8,128)(2,1)}, u32[]{:S(2)}) %copy-start.1) | copy-done | bytes 524312
  2.7 0.0 copy-start.2
  2.7 1.0 %copy-done.2 = bf16[512,512]{1,0:T(8,128)(2,1)S(1)} copy-done((bf16[512,512]{1,0:T(8,128)(2,1)S(1)}, bf16[512,512]{1,0:T(8,128)(2,1)}, u32[]{:S(2)}) %copy-start.2) | copy-done | bytes 524312
  3.8 0.0 copy-start.3
  3.8 1.0 %copy-done.3 = bf16[512,512]{1,0:T(8,128)(2,1)S(1)} copy-done((bf16[512,512]{1,0:T(8,128)(2,1)S(1)}, bf16[512,512]{1,0:T(8,128)(2,1)}, u32[]{:S(2)}) %copy-start.3) | copy-done | bytes 524312
  4.8 0.0 copy-start.4
  4.8 0.7 copy-done.4
  5.5 0.0 copy-start.5
  5.5 0.7 copy-done.5
  6.2 69.9 %lightning.1 = (bf16[512,512]{1,0:T(8,128)(2,1)S(1)}, bf16[512,512]{1,0:T(8,128)(2,1)S(1)}, bf16[512,512]{1,0:T(8,128)(2,1)S(1)}, bf16[512,512]{1,0:T(8,128)(2,1)S(1)}, f32[1,512]{1,0:T(1,128)S(1)}) custom-call(bf16[512,512]{1,0:T(8,128)(2,1)S(1)} %copy-done, bf16[512,512]{1,0:T(8,128)(2,1)S(1)} %copy-done.1, bf16[512,512]{1,0:T(8,128)(2,1)S(1)} %copy-done.2, ...), custom_call_target="tpu_custom_call" | custom-call | tf_op jit(solution)/shard_map/lightning/pallas_call | solution.py:462
  76.1 0.8 copy.16
  76.9 0.8 copy.17
  77.7 0.8 copy.18
  78.5 0.8 copy.19
  79.3 0.6 copy.20
Async XLA Ops:
  0.6 1.0 %copy-start = (bf16[512,512]{1,0:T(8,128)(2,1)S(1)}, bf16[512,512]{1,0:T(8,128)(2,1)}, u32[]{:S(2)}) copy-start(bf16[512,512]{1,0:T(8,128)(2,1)} %q_ref.1) | copy-start | bytes 1572868
  1.7 1.0 %copy-start.1 = (bf16[512,512]{1,0:T(8,128)(2,1)S(1)}, bf16[512,512]{1,0:T(8,128)(2,1)}, u32[]{:S(2)}) copy-start(bf16[512,512]{1,0:T(8,128)(2,1)} %k_ref.1) | copy-start | bytes 1572868
  2.7 1.0 %copy-start.2 = (bf16[512,512]{1,0:T(8,128)(2,1)S(1)}, bf16[512,512]{1,0:T(8,128)(2,1)}, u32[]{:S(2)}) copy-start(bf16[512,512]{1,0:T(8,128)(2,1)} %v_ref.1) | copy-start | bytes 1572868
  3.8 1.0 %copy-start.3 = (bf16[512,512]{1,0:T(8,128)(2,1)S(1)}, bf16[512,512]{1,0:T(8,128)(2,1)}, u32[]{:S(2)}) copy-start(bf16[512,512]{1,0:T(8,128)(2,1)} %go_ref.1) | copy-start | bytes 1572868
  4.8 0.7 copy-start.4
  5.5 0.7 copy-start.5

commit v2 on v1

--- a/solution.py
+++ b/solution.py
@@ -16,6 +16,7 @@
 ROWS = CHUNK * CHUNKS
 EXTRA = 8
 RING_X = 4
+VMEM_BYTES = 48 * 1024 * 1024
 
 NT = (((1,), (1,)), ((), ()))
 NN = (((1,), (0,)), ((), ()))
@@ -39,17 +40,24 @@
     n_ctx,
     n_dp,
     ring_x,
+    q_hbm,
+    k_hbm,
+    v_hbm,
+    decay_hbm,
+    gain_hbm,
+    go_hbm,
+    attended_ref,
+    gq_ref,
+    gk_ref,
+    gv_ref,
+    gg_ref,
     q_ref,
     k_ref,
     v_ref,
     decay_ref,
     gain_ref,
     go_ref,
-    attended_ref,
-    gq_ref,
-    gk_ref,
-    gv_ref,
-    gg_ref,
+    sem_in,
     rows_ref,
     cols_ref,
     gap_ref,
@@ -68,6 +76,8 @@
     recv_b,
     back_b,
     end_ref,
+    gain_out,
+    gain_in,
     sums_ref,
     norm_cols_ref,
     sems_f,
@@ -80,6 +90,8 @@
     semr_bb,
     sems_n,
     semr_n,
+    sems_g,
+    semr_g,
 ):
     me = lax.axis_index("ctx")
     col = lax.axis_index("dp")
@@ -87,14 +99,45 @@
     per_head = HEAD // piece
     ring_y = n_ctx // ring_x
     my_y, my_x = me // ring_x, me % ring_x
-
+    my_head = me // per_head
+    ring_z = n_dp // 2
+    far_x = sorted(range(ring_x), key=lambda d: -min(d, ring_x - d))
+
+    loads = [
+        pltpu.make_async_copy(source, target, sem_in.at[i])
+        for i, (source, target) in enumerate(
+            (
+                (decay_hbm, decay_ref),
+                (k_hbm, k_ref),
+                (v_hbm, v_ref),
+                (q_hbm, q_ref),
+                (gain_hbm, gain_ref),
+                (go_hbm, go_ref),
+            )
+        )
+    ]
+    for load in loads:
+        load.start()
     barrier = pltpu.get_barrier_semaphore()
 
-    def greet_ctx(i, carry):
+    def far_line(i):
+        step = ring_y // 2 + ((i + 1) // 2) * (1 - 2 * ((i + 1) % 2))
+        return ((my_y + step) % ring_y) * ring_x
+
+    def greet(there):
         pl.semaphore_signal(
-            barrier, inc=1, device_id={"ctx": (me + i) % n_ctx}, device_id_type=MESH
-        )
+            barrier, inc=1, device_id={"ctx": there}, device_id_type=MESH
+        )
+
+    def greet_line(i, carry):
+        line = far_line(i)
+        for step_x in far_x:
+            greet(line + (my_x + step_x) % ring_x)
         return carry
+
+    lax.fori_loop(0, ring_y - 1, greet_line, 0)
+    for step_x in far_x[:-1]:
+        greet(my_y * ring_x + (my_x + step_x) % ring_x)
 
     def greet_dp(i, carry):
         pl.semaphore_signal(
@@ -102,9 +145,9 @@
         )
         return carry
 
-    lax.fori_loop(1, n_ctx, greet_ctx, 0)
     lax.fori_loop(1, n_dp, greet_dp, 0)
 
+    loads[0].wait()
     logs = decay_ref[...]
     stacked = jnp.concatenate([logs[:, part(c)] for c in range(CHUNKS)], axis=0)
     high = stacked.astype(jnp.bfloat16)
@@ -136,6 +179,9 @@
         at = 16 * kind + c * HEADS_HERE + h
         return cols_ref[:, at : at + 1]
 
+    loads[1].wait()
+    loads[2].wait()
+
     for h in range(HEADS_HERE):
         weighted_keys = jnp.concatenate(
             [
@@ -153,62 +199,59 @@
         send_f[h * per_head : (h + 1) * per_head, piece:, :] = jnp.broadcast_to(
             total[h : h + 1][None], (per_head, EXTRA, HEAD)
         )
-    recv_f[pl.ds(me, 1)] = send_f[pl.ds(me, 1)]
-
     pl.semaphore_wait(barrier, n_ctx - 1 + n_dp - 1)
 
-    def far_first(i):
-        k, j = i // ring_x, i % ring_x
-        step_y = ring_y // 2 + ((k + 1) // 2) * (1 - 2 * ((k + 1) % 2))
-        step_x = ring_x // 2 + ((j + 1) // 2) * (1 - 2 * ((j + 1) % 2))
-        return ((my_y + step_y) % ring_y) * ring_x + (my_x + step_x) % ring_x
-
-    def out_copy(there, send, recv, ss, rs):
+    taken, given = pl.ds(0, piece + 1), pl.ds(0, piece)
+
+    def copy_to(there, rows, source, target, ss, rs):
         return pltpu.make_async_remote_copy(
-            src_ref=send.at[there],
-            dst_ref=recv.at[me],
-            send_sem=ss.at[there],
-            recv_sem=rs.at[me],
+            src_ref=source.at[there, rows],
+            dst_ref=target.at[me, rows],
+            send_sem=ss,
+            recv_sem=rs,
             device_id={"ctx": there},
             device_id_type=MESH,
         )
 
-    def in_copy(there, send, recv, ss, rs):
-        return pltpu.make_async_remote_copy(
-            src_ref=send.at[there],
-            dst_ref=recv.at[there],
-            send_sem=ss.at[there],
-            recv_sem=rs.at[there],
-            device_id={"ctx": there},
-            device_id_type=MESH,
-        )
-
-    def spread(send, recv, ss, rs):
+    def own_copy(rows, source, target, rs):
+        return pltpu.make_async_copy(source.at[me, rows], target.at[me, rows], rs)
+
+    def wait_group(first, count, rows, source, target, rs):
+        group = pl.ds(first, count)
+        pltpu.make_async_copy(
+            source.at[group, rows], target.at[group, rows], rs
+        ).wait()
+
+    def spread(source, target, ss, rs):
+        own_copy(taken, source, target, rs.at[my_y]).start()
+
         def one(i, carry):
-            out_copy(far_first(i), send, recv, ss, rs).start()
+            line = far_line(i)
+            for step_x in far_x:
+                there = line + (my_x + step_x) % ring_x
+                copy_to(there, taken, source, target, ss, rs.at[my_y]).start()
             return carry
 
-        lax.fori_loop(0, n_ctx - 1, one, 0)
-
-    def wait_sent(send, recv, ss, rs):
-        def one(i, carry):
-            there = (me + i) % n_ctx
-            in_copy(there, send, recv, ss, rs).wait_send()
-            return carry
-
-        lax.fori_loop(1, n_ctx, one, 0)
-
-    def wait_pieces(first, last, send, recv, ss, rs):
-        def one(there, carry):
-            @pl.when(there != me)
-            def _():
-                in_copy(there, send, recv, ss, rs).wait_recv()
-
-            return carry
-
-        lax.fori_loop(first, last, one, 0)
+        lax.fori_loop(0, ring_y - 1, one, 0)
+        for step_x in far_x[:-1]:
+            there = my_y * ring_x + (my_x + step_x) % ring_x
+            copy_to(there, taken, source, target, ss, rs.at[my_y]).start()
+
+    def give_back(there, running, source, target, ss, rs):
+        source[pl.ds(there, 1)] = running[None]
+
+        @pl.when(there != me)
+        def _():
+            copy_to(there, given, source, target, ss, rs.at[my_head]).start()
+
+        @pl.when(there == me)
+        def _():
+            own_copy(given, source, target, rs.at[my_head]).start()
 
     spread(send_f, recv_f, sems_f, semr_f)
+
+    for load in loads[3:]:
+        load.wait()
 
     diag_t = lax.broadcasted_iota(jnp.int32, (CHUNK, CHUNK), 0)
     diag_s = lax.broadcasted_iota(jnp.int32, (CHUNK, CHUNK), 1)
@@ -241,29 +284,24 @@
     forward_part(0)
     forward_part(1)
 
-    def scan_forward(there, running):
-        @pl.when(there != me)
-        def _():
-            in_copy(there, send_f, recv_f, sems_f, semr_f).wait_recv()
-
-        back_f[pl.ds(there, 1)] = running[None]
-
-        @pl.when(there != me)
-        def _():
-            out_copy(there, back_f, start_ref, sems_fb, semr_fb).start()
-
-        arrived = recv_f[pl.ds(there, 1)][0]
-        return jnp.exp(arrived[piece : piece + 1]) * running + arrived[:piece]
-
-    lax.fori_loop(0, n_ctx, scan_forward, jnp.zeros((piece, HEAD), jnp.float32))
-    start_ref[pl.ds(me, 1)] = back_f[pl.ds(me, 1)]
+    def scan_forward(line, running):
+        first = line * ring_x
+        wait_group(first, ring_x, taken, send_f, recv_f, semr_f.at[line])
+        for x in range(ring_x):
+            there = first + x
+            give_back(there, running, back_f, start_ref, sems_fb, semr_fb)
+            arrived = recv_f[pl.ds(there, 1)][0]
+            running = jnp.exp(arrived[piece : piece + 1]) * running + arrived[:piece]
+        return running
+
+    lax.fori_loop(0, ring_y, scan_forward, jnp.zeros((piece, HEAD), jnp.float32))
 
     forward_part(2)
     forward_part(3)
 
     for h in range(HEADS_HERE):
-        wait_pieces(
-            h * per_head, (h + 1) * per_head, back_f, start_ref, sems_fb, semr_fb
+        wait_group(
+            h * per_head, per_head, given, back_f, start_ref, semr_fb.at[h]
         )
         start = start_ref[h * per_head : (h + 1) * per_head].reshape(HEAD, HEAD)
         high, low = split(start)
@@ -301,25 +339,24 @@
         return pltpu.make_async_remote_copy(
             src_ref=sums_ref.at[slot],
             dst_ref=sums_ref.at[slot],
-            send_sem=sems_n.at[there],
-            recv_sem=semr_n.at[slot],
+            send_sem=sems_n,
+            recv_sem=semr_n,
             device_id={"dp": there},
             device_id_type=MESH,
         )
 
     def norm_send(i, carry):
-        norm_copy(col, (col + n_dp // 2 + i) % n_dp).start()
+        step = ring_z // 2 + ((i + 1) // 2) * (1 - 2 * ((i + 1) % 2))
+        level = ((col // 2 + step) % ring_z) * 2
+        for core in range(2):
+            norm_copy(col, level + core).start()
         return carry
 
-    def norm_wait(i, carry):
-        there = (col + i) % n_dp
-        norm_copy(there, there).wait_recv()
-        return carry
-
-    half = n_dp // 2
-    lax.fori_loop(0, half, norm_send, 0)
-    lax.fori_loop(half + 1, n_dp, norm_send, 0)
-    lax.fori_loop(1, n_dp, norm_wait, 0)
+    lax.fori_loop(0, ring_z - 1, norm_send, 0)
+    norm_copy(col, col + 1 - 2 * (col % 2)).start()
+    pltpu.make_async_copy(
+        sums_ref.at[pl.ds(0, n_dp - 1)], sums_ref.at[pl.ds(0, n_dp - 1)], semr_n
+    ).wait()
 
     both = jnp.sum(sums_ref[...], axis=0)
     features = HEAD * HEADS_HERE * n_dp
@@ -351,7 +388,6 @@
         send_b[h * per_head : (h + 1) * per_head, piece:, :] = jnp.broadcast_to(
             (gain_part * scale)[None], (per_head, EXTRA, HEAD)
         )
-    recv_b[pl.ds(me, 1)] = send_b[pl.ds(me, 1)]
     spread(send_b, recv_b, sems_b, semr_b)
 
     def backward_part(h):
@@ -384,45 +420,54 @@
 
     def scan_backward(i, carry):
         running, gain_sum = carry
-        there = n_ctx - 1 - i
-
-        @pl.when(there != me)
-        def _():
-            in_copy(there, send_b, recv_b, sems_b, semr_b).wait_recv()
-
-        back_b[pl.ds(there, 1), :piece] = running[None]
-        arrived = recv_b[pl.ds(there, 1)][0]
-        decay = jnp.exp(recv_f[pl.ds(there, 1)][0, piece : piece + 1])
-        return decay * running + arrived[:piece], gain_sum + arrived[piece:]
-
+        line = ring_y - 1 - i
+        first = line * ring_x
+        wait_group(first, ring_x, taken, send_b, recv_b, semr_b.at[line])
+        for x in reversed(range(ring_x)):
+            there = first + x
+            give_back(there, running, back_b, end_ref, sems_bb, semr_bb)
+            arrived = recv_b[pl.ds(there, 1)][0]
+            decay = jnp.exp(recv_f[pl.ds(there, 1)][0, piece : piece + 1])
+            running = decay * running + arrived[:piece]
+            gain_sum = gain_sum + arrived[piece : piece + 1]
+        return running, gain_sum
+
+    nothing = jnp.zeros((1, HEAD), jnp.float32)
     _, gain_sum = lax.fori_loop(
-        0,
-        n_ctx,
-        scan_backward,
-        (jnp.zeros((piece, HEAD), jnp.float32), jnp.zeros((EXTRA, HEAD), jnp.float32)),
+        0, ring_y, scan_backward, (jnp.zeros((piece, HEAD), jnp.float32), nothing)
     )
 
-    def gain_out(there, carry):
-        back_b[pl.ds(there, 1), piece:] = gain_sum[None]
-
-        @pl.when(there != me)
-        def _():
-            out_copy(there, back_b, end_ref, sems_bb, semr_bb).start()
-
-        return carry
-
-    lax.fori_loop(0, n_ctx, gain_out, 0)
-    end_ref[pl.ds(me, 1)] = back_b[pl.ds(me, 1)]
+    one_row = pl.ds(0, 1)
+
+    @pl.when(me % per_head == 0)
+    def _():
+        gain_out[...] = jnp.broadcast_to(gain_sum, (8, HEAD))
+        pltpu.make_async_copy(
+            gain_out.at[one_row], gain_in.at[my_head, one_row], semr_g
+        ).start()
+
+        def tell(i, carry):
+            pltpu.make_async_remote_copy(
+                src_ref=gain_out.at[one_row],
+                dst_ref=gain_in.at[my_head, one_row],
+                send_sem=sems_g,
+                recv_sem=semr_g,
+                device_id={"ctx": (me + n_ctx // 2 + i) % n_ctx},
+                device_id_type=MESH,
+            ).start()
+            return carry
+
+        lax.fori_loop(0, n_ctx // 2, tell, 0)
+        lax.fori_loop(n_ctx // 2 + 1, n_ctx, tell, 0)
 
     backward_part(2)
     backward_part(3)
 
     for h in range(HEADS_HERE):
-        wait_pieces(
-            h * per_head, (h + 1) * per_head, back_b, end_ref, sems_bb, semr_bb
-        )
-        end = end_ref[h * per_head : (h + 1) * per_head, :piece].reshape(HEAD, HEAD)
-        gg_ref[:, part(h)] = end_ref[h * per_head, piece : piece + 1]
+        wait_group(
+            h * per_head, per_head, given, back_b, end_ref, semr_bb.at[h]
+        )
+        end = end_ref[h * per_head : (h + 1) * per_head].reshape(HEAD, HEAD)
         high, low = split(end)
         for c in range(CHUNKS):
             values, keys = v_ref[part(c), part(h)], k_ref[part(c), part(h)]
@@ -436,17 +481,40 @@
                 fade * value_carried + lv_ref[part(c), part(h)]
             ).astype(jnp.bfloat16)
 
-    wait_sent(send_f, recv_f, sems_f, semr_f)
-    wait_sent(back_f, start_ref, sems_fb, semr_fb)
-    wait_sent(send_b, recv_b, sems_b, semr_b)
-    wait_sent(back_b, end_ref, sems_bb, semr_bb)
-
-    def norm_sent(i, carry):
-        there = (col + i) % n_dp
-        norm_copy(col, there).wait_send()
-        return carry
-
-    lax.fori_loop(1, n_dp, norm_sent, 0)
+    pltpu.make_async_copy(
+        gain_in.at[:, one_row], gain_in.at[:, one_row], semr_g
+    ).wait()
+    for h in range(HEADS_HERE):
+        gg_ref[:, part(h)] = gain_in[h, 0:1]
+
+    @pl.when(me % per_head == 0)
+    def _():
+        pltpu.make_async_copy(
+            recv_f.at[pl.ds(0, n_ctx - 1), one_row],
+            recv_b.at[pl.ds(0, n_ctx - 1), one_row],
+            sems_g,
+        ).wait()
+
+    wait_group(0, n_ctx - 1, taken, send_f, recv_f, sems_f)
+    wait_group(0, n_ctx - 1, given, back_f, start_ref, sems_fb)
+    wait_group(0, n_ctx - 1, taken, send_b, recv_b, sems_b)
+    wait_group(0, n_ctx - 1, given, back_b, end_ref, sems_bb)
+    pltpu.make_async_copy(
+        sums_ref.at[pl.ds(0, n_dp - 1)], sums_ref.at[pl.ds(0, n_dp - 1)], sems_n
+    ).wait()
+
+
+def store(*refs):
+    count = len(refs) // 2
+    sems = refs[-1]
+    copies = [
+        pltpu.make_async_copy(refs[i], refs[count + i], sems.at[i])
+        for i in range(count)
+    ]
+    for copy in copies:
+        copy.start()
+    for copy in copies:
+        copy.wait()
 
 
 def on_device(
@@ -459,12 +527,20 @@
     message = pltpu.VMEM((n_ctx, piece + EXTRA, HEAD), f32)
     plain = pltpu.VMEM((n_ctx, piece, HEAD), f32)
     vmem = pl.BlockSpec(memory_space=pltpu.VMEM)
+    hbm = pl.BlockSpec(memory_space=pltpu.HBM)
     outs = pl.pallas_call(
         functools.partial(kernel, n_ctx, n_dp, ring_x),
         out_shape=[full] * 4 + [jax.ShapeDtypeStruct((1, width), f32)],
-        in_specs=[vmem] * 6,
+        in_specs=[hbm] * 6,
         out_specs=[vmem] * 5,
         scratch_shapes=[
+            pltpu.VMEM((ROWS, width), bf16),
+            pltpu.VMEM((ROWS, width), bf16),
+            pltpu.VMEM((ROWS, width), bf16),
+            pltpu.VMEM((HEADS_HERE, ROWS), f32),
+            pltpu.VMEM((1, width), f32),
+            pltpu.VMEM((ROWS, width), bf16),
+            pltpu.SemaphoreType.DMA((6,)),
             pltpu.VMEM((16, CHUNK), f32),
             pltpu.VMEM((CHUNK, CHUNK), f32),
             pltpu.VMEM((HEADS_HERE, ROWS, ROWS), f32),
@@ -481,28 +557,50 @@
             plain,
             message,
             message,
-            message,
-            message,
+            plain,
+            plain,
+            pltpu.VMEM((8, HEAD), f32),
+            pltpu.VMEM((HEADS_HERE, 8, HEAD), f32),
             pltpu.VMEM((n_dp, 8, CHUNK), f32),
             pltpu.VMEM((CHUNK, CHUNK), f32),
         ]
-        + [pltpu.SemaphoreType.DMA((n_ctx,))] * 8
-        + [pltpu.SemaphoreType.DMA((n_dp,))] * 2,
+        + [
+            pltpu.SemaphoreType.DMA,
+            pltpu.SemaphoreType.DMA((n_ctx // ring_x,)),
+            pltpu.SemaphoreType.DMA,
+            pltpu.SemaphoreType.DMA((HEADS_HERE,)),
+        ]
+        * 2
+        + [pltpu.SemaphoreType.DMA] * 4,
         compiler_params=pltpu.CompilerParams(
             collective_id=0,
             has_side_effects=True,
-            vmem_limit_bytes=40 * 1024 * 1024,
+            vmem_limit_bytes=VMEM_BYTES,
         ),
         name="lightning",
     )(
-        query_in,
-        key_in,
-        value_in,
-        log_decay,
-        norm_gain.reshape(1, width),
-        grad_out,
+        *(
+            pltpu.with_memory_space_constraint(array, pltpu.HBM)
+            for array in (
+                query_in,
+                key_in,
+                value_in,
+                log_decay,
+                norm_gain.reshape(1, width),
+                grad_out,
+            )
+        )
     )
-    return (*outs[:4], outs[4].reshape(width))
+    stored = pl.pallas_call(
+        store,
+        out_shape=[full] * 4 + [jax.ShapeDtypeStruct((1, width), f32)],
+        in_specs=[vmem] * 5,
+        out_specs=[hbm] * 5,
+        scratch_shapes=[pltpu.SemaphoreType.DMA((5,))],
+        compiler_params=pltpu.CompilerParams(vmem_limit_bytes=1024 * 1024),
+        name="store",
+    )(*outs)
+    return (*stored[:4], stored[4].reshape(width))
 
 
 def solution(mesh):

time: 80.2 us -> 62.6 us (0.78)
  the two profiles are of different devices: /device:TPU:16 before, /device:TPU:1 now
where the time goes in v2:
time: 62.6 us; the launch traced here: 62.5 us
  Pallas kernels  61.9 us (99%)
  between operations  0.64 us (1%)
    pallas_call x1, Pallas kernels, on_device(): pl.pallas_call(functools.partial(kernel, n_ctx, n_dp, ring_x), out_shape=...  60.5 us
    pallas_call x1, Pallas kernels, on_device(): pl.pallas_call(store, out_shape=[full] * 4 + [jax.ShapeDtypeStruct((1, wi...  1.36 us

profile of v2, /device:TPU:1, one launch (start us, length us, event | category | flops | bytes accessed | tf_op | source)
XLA Modules:
  0.0 62.5 jit_solution(6883853312270766123)
XLA Ops:
  0.6 60.5 %lightning.1 = (bf16[512,512]{1,0:T(8,128)(2,1)S(1)}, bf16[512,512]{1,0:T(8,128)(2,1)S(1)}, bf16[512,512]{1,0:T(8,128)(2,1)S(1)}, bf16[512,512]{1,0:T(8,128)(2,1)S(1)}, f32[1,512]{1,0:T(1,128)S(1)}) custom-call(bf16[512,512]{1,0:T(8,128)(2,1)} %q_hbm.1, bf16[512,512]{1,0:T(8,128)(2,1)} %k_hbm.1, bf16[512,512]{1,0:T(8,128)(2,1)} %v_hbm.1, ...), custom_call_target="tpu_custom_call" | custom-call | tf_op jit(solution)/shard_map/lightning/pallas_call | solution.py:531
  61.1 1.4 %store.1 = (bf16[512,512]{1,0:T(8,128)(2,1)}, bf16[512,512]{1,0:T(8,128)(2,1)}, bf16[512,512]{1,0:T(8,128)(2,1)}, bf16[512,512]{1,0:T(8,128)(2,1)}, f32[1,512]{1,0:T(1,128)}) custom-call(bf16[512,512]{1,0:T(8,128)(2,1)S(1)} %get-tuple-element.15.refs_0_, bf16[512,512]{1,0:T(8,128)(2,1)S(1)} %get-tuple-element.16.refs_1_, ...), custom_call_target="tpu_custom_call" | custom-call | tf_op jit(solution)/shard_map/store/pallas_call | solution.py:594

commit v3 on v2

--- a/solution.py
+++ b/solution.py
@@ -25,11 +25,6 @@
 
 def mxu(left, right, form):
     return lax.dot_general(left, right, form, preferred_element_type=jnp.float32)
-
-
-def split(state):
-    high = state.astype(jnp.bfloat16)
-    return high, (state - high.astype(jnp.float32)).astype(jnp.bfloat16)
 
 
 def part(index):
@@ -48,26 +43,25 @@
     go_hbm,
     attended_ref,
     gq_ref,
-    gk_ref,
-    gv_ref,
     gg_ref,
-    q_ref,
     k_ref,
     v_ref,
+    cols_ref,
+    lk_ref,
+    lv_ref,
+    end_ref,
+    q_ref,
     decay_ref,
     gain_ref,
     go_ref,
     sem_in,
     rows_ref,
-    cols_ref,
     gap_ref,
     weighted_ref,
     gw_ref,
     mix_ref,
     g_ref,
     qw_ref,
-    lk_ref,
-    lv_ref,
     send_f,
     recv_f,
     back_f,
@@ -75,7 +69,6 @@
     send_b,
     recv_b,
     back_b,
-    end_ref,
     gain_out,
     gain_in,
     sums_ref,
@@ -237,6 +230,20 @@
             there = my_y * ring_x + (my_x + step_x) % ring_x
             copy_to(there, taken, source, target, ss, rs.at[my_y]).start()
 
+    def spread_head(h, source, target, ss, rs):
+        def one(there, carry):
+            @pl.when(there != me)
+            def _():
+                copy_to(there, taken, source, target, ss, rs.at[my_y]).start()
+
+            @pl.when(there == me)
+            def _():
+                own_copy(taken, source, target, rs.at[my_y]).start()
+
+            return carry
+
+        lax.fori_loop(h * per_head, (h + 1) * per_head, one, 0)
+
     def give_back(there, running, source, target, ss, rs):
         source[pl.ds(there, 1)] = running[None]
 
@@ -277,12 +284,11 @@
                 v_ref[: (i + 1) * CHUNK, part(h)],
                 NN,
             )
-            qw_ref[part(i), part(h)] = (
-                q_ref[part(i), part(h)].astype(jnp.float32) * column(1, h, i)
+            qw_ref[part(h), part(i)] = (
+                (q_ref[part(i), part(h)].astype(jnp.float32) * column(1, h, i)).T
             ).astype(jnp.bfloat16)
 
     forward_part(0)
-    forward_part(1)
 
     def scan_forward(line, running):
         first = line * ring_x
@@ -296,6 +302,7 @@
 
     lax.fori_loop(0, ring_y, scan_forward, jnp.zeros((piece, HEAD), jnp.float32))
 
+    forward_part(1)
     forward_part(2)
     forward_part(3)
 
@@ -304,10 +311,9 @@
             h * per_head, per_head, given, back_f, start_ref, semr_fb.at[h]
         )
         start = start_ref[h * per_head : (h + 1) * per_head].reshape(HEAD, HEAD)
-        high, low = split(start)
+        start = start.astype(jnp.bfloat16)
         for c in range(CHUNKS):
-            rows = q_ref[part(c), part(h)]
-            carried = mxu(rows, high, NN) + mxu(rows, low, NN)
+            carried = mxu(q_ref[part(c), part(h)], start, NN)
             mix_ref[part(c), part(h)] += column(1, h, c) * carried
 
     ones = jnp.ones((8, CHUNK), jnp.float32)
@@ -375,24 +381,29 @@
             grad = go_ref[part(c), part(h)].astype(jnp.float32)
             inv_c = norm_cols_ref[:, c : c + 1]
             bent_c = norm_cols_ref[:, CHUNKS + c : CHUNKS + c + 1]
-            normed = raw * inv_c
-            attended_ref[part(c), part(h)] = (normed * gain).astype(jnp.bfloat16)
-            gain_part += jnp.sum(grad * normed, axis=0, keepdims=True)
-            g_ref[part(c), part(h)] = (inv_c * (grad * gain) - raw * bent_c).astype(
-                jnp.bfloat16
-            )
-        back = mxu(qw_ref[:, part(h)], g_ref[:, part(h)], TN)
+            even = grad * inv_c
+            gain_part += jnp.sum(even * raw, axis=0, keepdims=True)
+            g_ref[part(c), part(h)] = (even * gain - raw * bent_c).astype(jnp.bfloat16)
+        back = mxu(qw_ref[part(h), :], g_ref[:, part(h)], NN)
         send_b[h * per_head : (h + 1) * per_head, :piece, :] = back.reshape(
             per_head, piece, HEAD
         )
         send_b[h * per_head : (h + 1) * per_head, piece:, :] = jnp.broadcast_to(
             (gain_part * scale)[None], (per_head, EXTRA, HEAD)
         )
-    spread(send_b, recv_b, sems_b, semr_b)
+        spread_head(h, send_b, recv_b, sems_b, semr_b)
+
+    for h in range(HEADS_HERE):
+        for c in range(CHUNKS):
+            attended_ref[part(c), part(h)] = (
+                mix_ref[part(c), part(h)]
+                * norm_cols_ref[:, c : c + 1]
+                * gain_ref[:, part(h)]
+            ).astype(jnp.bfloat16)
 
     def backward_part(h):
         start = start_ref[h * per_head : (h + 1) * per_head].reshape(HEAD, HEAD)
-        high, low = split(start)
+        start = start.astype(jnp.bfloat16)
         for i in range(CHUNKS):
             upto = slice(0, (i + 1) * CHUNK)
             rows = g_ref[part(i), part(h)]
@@ -402,7 +413,7 @@
                     scores[:, part(j)] * gap_ref[h, part(i), part(j)]
                 ).astype(jnp.bfloat16)
             local = mxu(gw_ref[h, part(i), upto], k_ref[upto, part(h)], NN)
-            carried = mxu(rows, high, NT) + mxu(rows, low, NT)
+            carried = mxu(rows, start, NT)
             gq_ref[part(i), part(h)] = (column(1, h, i) * carried + local).astype(
                 jnp.bfloat16
             )
@@ -467,20 +478,6 @@
         wait_group(
             h * per_head, per_head, given, back_b, end_ref, semr_bb.at[h]
         )
-        end = end_ref[h * per_head : (h + 1) * per_head].reshape(HEAD, HEAD)
-        high, low = split(end)
-        for c in range(CHUNKS):
-            values, keys = v_ref[part(c), part(h)], k_ref[part(c), part(h)]
-            fade = column(2, h, c)
-            key_carried = mxu(values, high, NT) + mxu(values, low, NT)
-            value_carried = mxu(keys, high, NN) + mxu(keys, low, NN)
-            gk_ref[part(c), part(h)] = (
-                fade * key_carried + lk_ref[part(c), part(h)]
-            ).astype(jnp.bfloat16)
-            gv_ref[part(c), part(h)] = (
-                fade * value_carried + lv_ref[part(c), part(h)]
-            ).astype(jnp.bfloat16)
-
     pltpu.make_async_copy(
         gain_in.at[:, one_row], gain_in.at[:, one_row], semr_g
     ).wait()
@@ -504,15 +501,55 @@
     ).wait()
 
 
-def store(*refs):
-    count = len(refs) // 2
-    sems = refs[-1]
+def finish(
+    attended_ref,
+    gq_ref,
+    gg_ref,
+    k_ref,
+    v_ref,
+    cols_ref,
+    lk_ref,
+    lv_ref,
+    end_ref,
+    attended_out,
+    gq_out,
+    gk_out,
+    gv_out,
+    gg_out,
+    gk_ref,
+    gv_ref,
+    sems,
+):
     copies = [
-        pltpu.make_async_copy(refs[i], refs[count + i], sems.at[i])
-        for i in range(count)
+        pltpu.make_async_copy(source, target, sems.at[i])
+        for i, (source, target) in enumerate(
+            ((attended_ref, attended_out), (gq_ref, gq_out), (gg_ref, gg_out))
+        )
     ]
     for copy in copies:
         copy.start()
+    piece = end_ref.shape[1]
+    per_head = HEAD // piece
+    for c in range(CHUNKS):
+        for h in range(HEADS_HERE):
+            end = end_ref[h * per_head : (h + 1) * per_head].reshape(HEAD, HEAD)
+            end = end.astype(jnp.bfloat16)
+            at = 32 + c * HEADS_HERE + h
+            fade = cols_ref[:, at : at + 1]
+            gk_ref[part(c), part(h)] = (
+                fade * mxu(v_ref[part(c), part(h)], end, NT)
+                + lk_ref[part(c), part(h)]
+            ).astype(jnp.bfloat16)
+            gv_ref[part(c), part(h)] = (
+                fade * mxu(k_ref[part(c), part(h)], end, NN)
+                + lv_ref[part(c), part(h)]
+            ).astype(jnp.bfloat16)
+        for i, (source, target) in enumerate(((gk_ref, gk_out), (gv_ref, gv_out))):
+            copy = pltpu.make_async_copy(
+                source.at[part(c)], target.at[part(c)], sems.at[3 + 2 * c + i]
+            )
+            copy.start()
+            copies.append(copy)
     for copy in copies:
         copy.wait()
 
@@ -530,34 +567,38 @@
     hbm = pl.BlockSpec(memory_space=pltpu.HBM)
     outs = pl.pallas_call(
         functools.partial(kernel, n_ctx, n_dp, ring_x),
-        out_shape=[full] * 4 + [jax.ShapeDtypeStruct((1, width), f32)],
+        out_shape=[
+            full,
+            full,
+            jax.ShapeDtypeStruct((1, width), f32),
+            full,
+            full,
+            jax.ShapeDtypeStruct((CHUNK, CHUNK), f32),
+            jax.ShapeDtypeStruct((ROWS, width), f32),
+            jax.ShapeDtypeStruct((ROWS, width), f32),
+            jax.ShapeDtypeStruct((n_ctx, piece, HEAD), f32),
+        ],
         in_specs=[hbm] * 6,
-        out_specs=[vmem] * 5,
+        out_specs=[vmem] * 9,
         scratch_shapes=[
-            pltpu.VMEM((ROWS, width), bf16),
-            pltpu.VMEM((ROWS, width), bf16),
             pltpu.VMEM((ROWS, width), bf16),
             pltpu.VMEM((HEADS_HERE, ROWS), f32),
             pltpu.VMEM((1, width), f32),
             pltpu.VMEM((ROWS, width), bf16),
             pltpu.SemaphoreType.DMA((6,)),
             pltpu.VMEM((16, CHUNK), f32),
-            pltpu.VMEM((CHUNK, CHUNK), f32),
             pltpu.VMEM((HEADS_HERE, ROWS, ROWS), f32),
             pltpu.VMEM((HEADS_HERE, ROWS, ROWS), bf16),
             pltpu.VMEM((HEADS_HERE, ROWS, ROWS), bf16),
             pltpu.VMEM((ROWS, width), f32),
             pltpu.VMEM((ROWS, width), bf16),
-            pltpu.VMEM((ROWS, width), bf16),
-            pltpu.VMEM((ROWS, width), f32),
-            pltpu.VMEM((ROWS, width), f32),
+            pltpu.VMEM((width, ROWS), bf16),
             message,
             message,
             plain,
             plain,
             message,
             message,
-            plain,
             plain,
             pltpu.VMEM((8, HEAD), f32),
             pltpu.VMEM((HEADS_HERE, 8, HEAD), f32),
@@ -592,13 +633,17 @@
         )
     )
     stored = pl.pallas_call(
-        store,
+        finish,
         out_shape=[full] * 4 + [jax.ShapeDtypeStruct((1, width), f32)],
-        in_specs=[vmem] * 5,
+        in_specs=[vmem] * 9,
         out_specs=[hbm] * 5,
-        scratch_shapes=[pltpu.SemaphoreType.DMA((5,))],
-        compiler_params=pltpu.CompilerParams(vmem_limit_bytes=1024 * 1024),
-        name="store",
+        scratch_shapes=[
+            pltpu.VMEM((ROWS, width), bf16),
+            pltpu.VMEM((ROWS, width), bf16),
+            pltpu.SemaphoreType.DMA((3 + 2 * CHUNKS,)),
+        ],
+        compiler_params=pltpu.CompilerParams(vmem_limit_bytes=4 * 1024 * 1024),
+        name="finish",
     )(*outs)
     return (*stored[:4], stored[4].reshape(width))
 

time: 62.6 us -> 61.5 us (0.982)
  Pallas kernels: 61.9 us -> 60.2 us
    pallas_call x1, Pallas kernels: 60.5 us -> 58.8 us  [on_device(): pl.pallas_call(functools.partial(kernel, n_ctx, n_dp, ring_x), out_shape=...]
where the time goes in v3:
time: 61.5 us; the launch traced here: 60.9 us
  Pallas kernels  60.2 us (98%)
  between operations  0.64 us (1%)
    pallas_call x1, Pallas kernels, on_device(): pl.pallas_call(functools.partial(kernel, n_ctx, n_dp, ring_x), out_shape=...  58.8 us
    pallas_call x1, Pallas kernels, on_device(): pl.pallas_call(finish, out_shape=[full] * 4 + [jax.ShapeDtypeStruct((1, w...  1.4 us

profile of v3, /device:TPU:1, one launch (start us, length us, event | category | flops | bytes accessed | tf_op | source)
XLA Modules:
  0.0 60.9 jit_solution(15286836378882336110)
XLA Ops:
  0.6 58.8 %lightning.1 = (bf16[512,512]{1,0:T(8,128)(2,1)S(1)}, bf16[512,512]{1,0:T(8,128)(2,1)S(1)}, f32[1,512]{1,0:T(1,128)S(1)}, bf16[512,512]{1,0:T(8,128)(2,1)S(1)}, ...) custom-call(bf16[512,512]{1,0:T(8,128)(2,1)} %q_hbm.1, ...), custom_call_target="tpu_custom_call" | custom-call | tf_op jit(solution)/shard_map/lightning/pallas_call | solution.py:568
  59.5 1.4 %finish.1 = (bf16[512,512]{1,0:T(8,128)(2,1)}, bf16[512,512]{1,0:T(8,128)(2,1)}, bf16[512,512]{1,0:T(8,128)(2,1)}, bf16[512,512]{1,0:T(8,128)(2,1)}, f32[1,512]{1,0:T(1,128)}) custom-call(bf16[512,512]{1,0:T(8,128)(2,1)S(1)} %get-tuple-element.19.attended_ref, bf16[512,512]{1,0:T(8,128)(2,1)S(1)} %get-tuple-element.20.gq_ref, ...), custom_call_target="tpu_custom_call" | custom-call | tf_op jit(solution)/shard_map/finish/pallas_call | solution.py:635

commit v4 on v3

--- a/solution.py
+++ b/solution.py
@@ -25,6 +25,11 @@
 
 def mxu(left, right, form):
     return lax.dot_general(left, right, form, preferred_element_type=jnp.float32)
+
+
+def split(terms):
+    high = terms.astype(jnp.bfloat16)
+    return high, (terms - high.astype(jnp.float32)).astype(jnp.bfloat16)
 
 
 def part(index):
@@ -89,6 +94,7 @@
     me = lax.axis_index("ctx")
     col = lax.axis_index("dp")
     piece = ROWS // n_ctx
+    half = piece // 2
     per_head = HEAD // piece
     ring_y = n_ctx // ring_x
     my_y, my_x = me // ring_x, me % ring_x
@@ -175,6 +181,15 @@
     loads[1].wait()
     loads[2].wait()
 
+    def fill(target, h, state, extra):
+        pieces = pl.ds(h * per_head, per_head)
+        state = state.reshape(per_head, 2, half, HEAD)
+        target[pieces, :half, :] = state[:, 0]
+        target[pieces, half : half + EXTRA, :] = jnp.broadcast_to(
+            extra[None], (per_head, EXTRA, HEAD)
+        )
+        target[pieces, half + EXTRA :, :] = state[:, 1]
+
     for h in range(HEADS_HERE):
         weighted_keys = jnp.concatenate(
             [
@@ -186,15 +201,12 @@
             axis=0,
         )
         state = mxu(weighted_keys, v_ref[:, part(h)], TN)
-        send_f[h * per_head : (h + 1) * per_head, :piece, :] = state.reshape(
-            per_head, piece, HEAD
-        )
-        send_f[h * per_head : (h + 1) * per_head, piece:, :] = jnp.broadcast_to(
-            total[h : h + 1][None], (per_head, EXTRA, HEAD)
-        )
+        fill(send_f, h, state, total[h : h + 1])
     pl.semaphore_wait(barrier, n_ctx - 1 + n_dp - 1)
 
     taken, given = pl.ds(0, piece + 1), pl.ds(0, piece)
+    taken_half = (pl.ds(0, half + 1), pl.ds(half + EXTRA, half))
+    given_half = (pl.ds(0, half), pl.ds(half, half))
 
     def copy_to(there, rows, source, target, ss, rs):
         return pltpu.make_async_remote_copy(
@@ -215,47 +227,52 @@
             source.at[group, rows], target.at[group, rows], rs
         ).wait()
 
-    def spread(source, target, ss, rs):
-        own_copy(taken, source, target, rs.at[my_y]).start()
+    def spread(which, source, target, ss, rs):
+        rows, arrival = taken_half[which], rs.at[which * ring_y + my_y]
+        own_copy(rows, source, target, arrival).start()
 
         def one(i, carry):
             line = far_line(i)
             for step_x in far_x:
                 there = line + (my_x + step_x) % ring_x
-                copy_to(there, taken, source, target, ss, rs.at[my_y]).start()
+                copy_to(there, rows, source, target, ss, arrival).start()
             return carry
 
         lax.fori_loop(0, ring_y - 1, one, 0)
         for step_x in far_x[:-1]:
             there = my_y * ring_x + (my_x + step_x) % ring_x
-            copy_to(there, taken, source, target, ss, rs.at[my_y]).start()
+            copy_to(there, rows, source, target, ss, arrival).start()
 
     def spread_head(h, source, target, ss, rs):
+        rows, arrival = taken_half[0], rs.at[my_y]
+
         def one(there, carry):
             @pl.when(there != me)
             def _():
-                copy_to(there, taken, source, target, ss, rs.at[my_y]).start()
+                copy_to(there, rows, source, target, ss, arrival).start()
 
             @pl.when(there == me)
             def _():
-                own_copy(taken, source, target, rs.at[my_y]).start()
+                own_copy(rows, source, target, arrival).start()
 
             return carry
 
         lax.fori_loop(h * per_head, (h + 1) * per_head, one, 0)
 
-    def give_back(there, running, source, target, ss, rs):
-        source[pl.ds(there, 1)] = running[None]
+    def give_back(which, there, running, source, target, ss, rs):
+        rows = given_half[which]
+        source[pl.ds(there, 1), rows] = running[None]
 
         @pl.when(there != me)
         def _():
-            copy_to(there, given, source, target, ss, rs.at[my_head]).start()
+            copy_to(there, rows, source, target, ss, rs.at[my_head]).start()
 
         @pl.when(there == me)
         def _():
-            own_copy(given, source, target, rs.at[my_head]).start()
-
-    spread(send_f, recv_f, sems_f, semr_f)
+            own_copy(rows, source, target, rs.at[my_head]).start()
+
+    spread(0, send_f, recv_f, sems_f, semr_f)
+    spread(1, send_f, recv_f, sems_f, semr_f)
 
     for load in loads[3:]:
         load.wait()
@@ -290,17 +307,26 @@
 
     forward_part(0)
 
-    def scan_forward(line, running):
+    def half_rows(source, there, which):
+        return source[pl.ds(there, 1), pl.ds(which * (half + EXTRA), half)][0]
+
+    def extra_row(source, there):
+        return source[pl.ds(there, 1), pl.ds(half, 1)][0]
+
+    def scan_forward(which, line, running):
         first = line * ring_x
-        wait_group(first, ring_x, taken, send_f, recv_f, semr_f.at[line])
+        arrival = semr_f.at[which * ring_y + line]
+        wait_group(first, ring_x, taken_half[which], send_f, recv_f, arrival)
         for x in range(ring_x):
             there = first + x
-            give_back(there, running, back_f, start_ref, sems_fb, semr_fb)
-            arrived = recv_f[pl.ds(there, 1)][0]
-            running = jnp.exp(arrived[piece : piece + 1]) * running + arrived[:piece]
+            give_back(which, there, running, back_f, start_ref, sems_fb, semr_fb)
+            decay = jnp.exp(extra_row(recv_f, there))
+            running = decay * running + half_rows(recv_f, there, which)
         return running
 
-    lax.fori_loop(0, ring_y, scan_forward, jnp.zeros((piece, HEAD), jnp.float32))
+    zero = jnp.zeros((half, HEAD), jnp.float32)
+    for which in range(2):
+        lax.fori_loop(0, ring_y, functools.partial(scan_forward, which), zero)
 
     forward_part(1)
     forward_part(2)
@@ -315,17 +341,6 @@
         for c in range(CHUNKS):
             carried = mxu(q_ref[part(c), part(h)], start, NN)
             mix_ref[part(c), part(h)] += column(1, h, c) * carried
-
-    ones = jnp.ones((8, CHUNK), jnp.float32)
-
-    def row_sums(terms):
-        return lax.dot_general(
-            ones,
-            terms,
-            NT,
-            preferred_element_type=jnp.float32,
-            precision=lax.Precision.HIGHEST,
-        )[0:1]
 
     squares, crosses = [], []
     for c in range(CHUNKS):
@@ -337,9 +352,13 @@
             cross += (
                 go_ref[part(c), part(h)].astype(jnp.float32) * gain_ref[:, part(h)]
             ) * raw
-        squares.append(row_sums(square))
-        crosses.append(row_sums(cross))
-    sums_ref[pl.ds(col, 1)] = jnp.concatenate(squares + crosses, axis=0)[None]
+        squares.append(jnp.concatenate(split(square), axis=1))
+        crosses.append(jnp.concatenate(split(cross), axis=1))
+    ones = jnp.ones((16, 2 * HEAD), jnp.bfloat16)
+    row_sums = mxu(ones, jnp.concatenate(squares + crosses, axis=0), NT)[0:1]
+    sums_ref[pl.ds(col, 1)] = jnp.concatenate(
+        [row_sums[:, part(c)] for c in range(2 * CHUNKS)], axis=0
+    )[None]
 
     def norm_copy(slot, there):
         return pltpu.make_async_remote_copy(
@@ -385,13 +404,9 @@
             gain_part += jnp.sum(even * raw, axis=0, keepdims=True)
             g_ref[part(c), part(h)] = (even * gain - raw * bent_c).astype(jnp.bfloat16)
         back = mxu(qw_ref[part(h), :], g_ref[:, part(h)], NN)
-        send_b[h * per_head : (h + 1) * per_head, :piece, :] = back.reshape(
-            per_head, piece, HEAD
-        )
-        send_b[h * per_head : (h + 1) * per_head, piece:, :] = jnp.broadcast_to(
-            (gain_part * scale)[None], (per_head, EXTRA, HEAD)
-        )
+        fill(send_b, h, back, gain_part * scale)
         spread_head(h, send_b, recv_b, sems_b, semr_b)
+    spread(1, send_b, recv_b, sems_b, semr_b)
 
     for h in range(HEADS_HERE):
         for c in range(CHUNKS):
@@ -429,24 +444,26 @@
     backward_part(0)
     backward_part(1)
 
-    def scan_backward(i, carry):
+    def scan_backward(which, i, carry):
         running, gain_sum = carry
         line = ring_y - 1 - i
         first = line * ring_x
-        wait_group(first, ring_x, taken, send_b, recv_b, semr_b.at[line])
+        arrival = semr_b.at[which * ring_y + line]
+        wait_group(first, ring_x, taken_half[which], send_b, recv_b, arrival)
         for x in reversed(range(ring_x)):
             there = first + x
-            give_back(there, running, back_b, end_ref, sems_bb, semr_bb)
-            arrived = recv_b[pl.ds(there, 1)][0]
-            decay = jnp.exp(recv_f[pl.ds(there, 1)][0, piece : piece + 1])
-            running = decay * running + arrived[:piece]
-            gain_sum = gain_sum + arrived[piece : piece + 1]
+            give_back(which, there, running, back_b, end_ref, sems_bb, semr_bb)
+            decay = jnp.exp(extra_row(recv_f, there))
+            running = decay * running + half_rows(recv_b, there, which)
+            gain_sum = gain_sum + extra_row(recv_b, there)
         return running, gain_sum
 
-    nothing = jnp.zeros((1, HEAD), jnp.float32)
-    _, gain_sum = lax.fori_loop(
-        0, ring_y, scan_backward, (jnp.zeros((piece, HEAD), jnp.float32), nothing)
-    )
+    sums = []
+    for which in range(2):
+        turn = functools.partial(scan_backward, which)
+        nothing = jnp.zeros((1, HEAD), jnp.float32)
+        sums.append(lax.fori_loop(0, ring_y, turn, (zero, nothing))[1])
+    gain_sum = sums[0]
 
     one_row = pl.ds(0, 1)
 
@@ -607,7 +624,7 @@
         ]
         + [
             pltpu.SemaphoreType.DMA,
-            pltpu.SemaphoreType.DMA((n_ctx // ring_x,)),
+            pltpu.SemaphoreType.DMA((2 * n_ctx // ring_x,)),
             pltpu.SemaphoreType.DMA,
             pltpu.SemaphoreType.DMA((HEADS_HERE,)),
         ]

time: 61.5 us -> 57.9 us (0.941)
  Pallas kernels: 60.2 us -> 57 us
    pallas_call x1, Pallas kernels: 58.8 us -> 55.6 us  [on_device(): pl.pallas_call(functools.partial(kernel, n_ctx, n_dp, ring_x), out_shape=...]
where the time goes in v4:
time: 57.9 us; the launch traced here: 57.6 us
  Pallas kernels  57 us (98%)
  between operations  0.64 us (1%)
    pallas_call x1, Pallas kernels, on_device(): pl.pallas_call(functools.partial(kernel, n_ctx, n_dp, ring_x), out_shape=...  55.6 us
    pallas_call x1, Pallas kernels, on_device(): pl.pallas_call(finish, out_shape=[full] * 4 + [jax.ShapeDtypeStruct((1, w...  1.4 us

profile of v4, /device:TPU:1, one launch (start us, length us, event | category | flops | bytes accessed | tf_op | source)
XLA Modules:
  0.0 57.6 jit_solution(16515370094807521111)
XLA Ops:
  0.6 55.6 %lightning.1 = (bf16[512,512]{1,0:T(8,128)(2,1)S(1)}, bf16[512,512]{1,0:T(8,128)(2,1)S(1)}, f32[1,512]{1,0:T(1,128)S(1)}, bf16[512,512]{1,0:T(8,128)(2,1)S(1)}, ...) custom-call(bf16[512,512]{1,0:T(8,128)(2,1)} %q_hbm.1, ...), custom_call_target="tpu_custom_call" | custom-call | tf_op jit(solution)/shard_map/lightning/pallas_call | solution.py:585
  56.2 1.4 %finish.1 = (bf16[512,512]{1,0:T(8,128)(2,1)}, bf16[512,512]{1,0:T(8,128)(2,1)}, bf16[512,512]{1,0:T(8,128)(2,1)}, bf16[512,512]{1,0:T(8,128)(2,1)}, f32[1,512]{1,0:T(1,128)}) custom-call(bf16[512,512]{1,0:T(8,128)(2,1)S(1)} %get-tuple-element.19.attended_ref, bf16[512,512]{1,0:T(8,128)(2,1)S(1)} %get-tuple-element.20.gq_ref, ...), custom_call_target="tpu_custom_call" | custom-call | tf_op jit(solution)/shard_map/finish/pallas_call | solution.py:652

commit v5 on v4

--- a/solution.py
+++ b/solution.py
@@ -458,35 +458,44 @@
             gain_sum = gain_sum + extra_row(recv_b, there)
         return running, gain_sum
 
-    sums = []
-    for which in range(2):
-        turn = functools.partial(scan_backward, which)
-        nothing = jnp.zeros((1, HEAD), jnp.float32)
-        sums.append(lax.fori_loop(0, ring_y, turn, (zero, nothing))[1])
-    gain_sum = sums[0]
-
     one_row = pl.ds(0, 1)
-
-    @pl.when(me % per_head == 0)
-    def _():
-        gain_out[...] = jnp.broadcast_to(gain_sum, (8, HEAD))
-        pltpu.make_async_copy(
-            gain_out.at[one_row], gain_in.at[my_head, one_row], semr_g
-        ).start()
-
-        def tell(i, carry):
+    told = n_ctx // per_head
+    tells_itself = me // told == me % per_head
+
+    def tell(i, carry):
+        there = (me % per_head) * told + i
+        source, target = gain_out.at[one_row], gain_in.at[my_head, one_row]
+
+        @pl.when(there != me)
+        def _():
             pltpu.make_async_remote_copy(
-                src_ref=gain_out.at[one_row],
-                dst_ref=gain_in.at[my_head, one_row],
+                src_ref=source,
+                dst_ref=target,
                 send_sem=sems_g,
                 recv_sem=semr_g,
-                device_id={"ctx": (me + n_ctx // 2 + i) % n_ctx},
+                device_id={"ctx": there},
                 device_id_type=MESH,
             ).start()
-            return carry
-
-        lax.fori_loop(0, n_ctx // 2, tell, 0)
-        lax.fori_loop(n_ctx // 2 + 1, n_ctx, tell, 0)
+
+        @pl.when(there == me)
+        def _():
+            pltpu.make_async_copy(source, target, semr_g).start()
+
+        return carry
+
+    def wait_told(count):
+        rows = pl.ds(0, count)
+        pltpu.make_async_copy(
+            recv_f.at[rows, one_row], recv_b.at[rows, one_row], sems_g
+        ).wait()
+
+    nothing = jnp.zeros((1, HEAD), jnp.float32)
+    turn = functools.partial(scan_backward, 0)
+    _, gain_sum = lax.fori_loop(0, ring_y, turn, (zero, nothing))
+    gain_out[...] = jnp.broadcast_to(gain_sum, (8, HEAD))
+    lax.fori_loop(0, told, tell, 0)
+    turn = functools.partial(scan_backward, 1)
+    lax.fori_loop(0, ring_y, turn, (zero, nothing))
 
     backward_part(2)
     backward_part(3)
@@ -501,13 +510,13 @@
     for h in range(HEADS_HERE):
         gg_ref[:, part(h)] = gain_in[h, 0:1]
 
-    @pl.when(me % per_head == 0)
+    @pl.when(tells_itself)
     def _():
-        pltpu.make_async_copy(
-            recv_f.at[pl.ds(0, n_ctx - 1), one_row],
-            recv_b.at[pl.ds(0, n_ctx - 1), one_row],
-            sems_g,
-        ).wait()
+        wait_told(told - 1)
+
+    @pl.when(jnp.logical_not(tells_itself))
+    def _():
+        wait_told(told)
 
     wait_group(0, n_ctx - 1, taken, send_f, recv_f, sems_f)
     wait_group(0, n_ctx - 1, given, back_f, start_ref, sems_fb)

time: 57.9 us -> 57.9 us (level)
  no operation moved by 1% of the time
where the time goes in v5:
time: 57.9 us; the launch traced here: 57.6 us
  Pallas kernels  57 us (98%)
  between operations  0.64 us (1%)
    pallas_call x1, Pallas kernels, on_device(): pl.pallas_call(functools.partial(kernel, n_ctx, n_dp, ring_x), out_shape=...  55.6 us
    pallas_call x1, Pallas kernels, on_device(): pl.pallas_call(finish, out_shape=[full] * 4 + [jax.ShapeDtypeStruct((1, w...  1.4 us

profile of v5, /device:TPU:1, one launch (start us, length us, event | category | flops | bytes accessed | tf_op | source)
XLA Modules:
  0.0 57.6 jit_solution(8007633184189531406)
XLA Ops:
  0.6 55.6 %lightning.1 = (bf16[512,512]{1,0:T(8,128)(2,1)S(1)}, bf16[512,512]{1,0:T(8,128)(2,1)S(1)}, f32[1,512]{1,0:T(1,128)S(1)}, bf16[512,512]{1,0:T(8,128)(2,1)S(1)}, ...) custom-call(bf16[512,512]{1,0:T(8,128)(2,1)} %q_hbm.1, ...), custom_call_target="tpu_custom_call" | custom-call | tf_op jit(solution)/shard_map/lightning/pallas_call | solution.py:594
  56.2 1.4 %finish.1 = (bf16[512,512]{1,0:T(8,128)(2,1)}, bf16[512,512]{1,0:T(8,128)(2,1)}, bf16[512,512]{1,0:T(8,128)(2,1)}, bf16[512,512]{1,0:T(8,128)(2,1)}, f32[1,512]{1,0:T(1,128)}) custom-call(bf16[512,512]{1,0:T(8,128)(2,1)S(1)} %get-tuple-element.19.attended_ref, bf16[512,512]{1,0:T(8,128)(2,1)S(1)} %get-tuple-element.20.gq_ref, ...), custom_call_target="tpu_custom_call" | custom-call | tf_op jit(solution)/shard_map/finish/pallas_call | solution.py:661
